TPU v7x, 32 devices: a whole 2x2x4 slice. The times are simulated.
32 devices in a mesh: dev: 32 (over z, y, x, core).
Axes of the slice: x: 2, y: 2, z: 4, core: 2. Of those that a mesh axis runs over, the one named last changes fastest.
Arguments:
- velocity: float32 [256, 64, 256], P('dev'), may hold values from 1.5 to 4.5
- wave_prev: float32 [1024, 32, 128], P('dev')
- wave_now: float32 [1024, 32, 128], P('dev')
- adjoint_next: float32 [1024, 32, 128], P('dev'), may hold values from -6 to 6
- adjoint_now: float32 [1024, 32, 128], P('dev'), may hold values from -6 to 6
- wavelet: float32 [32, 2], P('dev'), may hold values from -12 to 12
- source_pos: int32 [32, 3], P('dev'), may hold values from 0 to 31, as said below
- cover_start: int32 [32], replicated, may hold values from 0 to 28, as said below
- lateral_anchor: int32 [32, 2], replicated, may hold values from 0 to 128, as said below
Outputs:
- wave_last: float32 [1024, 32, 128], P('dev')
- adjoint_last: float32 [1024, 32, 128], P('dev')
- gradient: float32 [256, 64, 256], P('dev')
Inputs may be any that keep to these rules, and one draw needn't show every extreme that they name: Aperture a covers the 4 slabs from cover_start[a] on, and its own slab a is among them. `lateral_anchor`: first entry at most 32, second at most 128. `source_pos`: every coordinate is below the smallest of 32, 32 and 128.
All inputs are finite; a program needn't handle non-finite values. Where the computation divides by a largest or mean magnitude, that divisor is 1e-20 or more.
Results may differ from a plain program's by a relative error of at most 0.00002.
Values sent between devices are 32-bit elements; how exact they have to be, the bound alone decides.
A program may use at most 64 MiB of HBM per device.

v0:
```python
import jax
import jax.numpy as jnp
from jax import lax
from jax.sharding import PartitionSpec as P

SLAB = 8
K = 4
AX = 32
AY = 128
AZ = 32
MX = 64
MY = 256


STENCIL_WEIGHTS = (-205.0 / 72.0, 8.0 / 5.0, -1.0 / 5.0, 8.0 / 315.0, -1.0 / 560.0)
STEP_RATIO = 0.088
EPSILON = 1e-06


def passed_along(value, axis, steps):
    count = lax.axis_size(axis)
    initial, last = (max(0, -steps), min(count, count - steps))
    return lax.ppermute(value, axis, [(source, source + steps) for source in range(initial, last)])


def laplace(wavefield):
    depth_cells, cross_cells, along_cells = wavefield.shape
    padded = jnp.pad(wavefield, 4)
    summed = 3.0 * STENCIL_WEIGHTS[0] * wavefield
    for distance in range(1, 5):
        weight = STENCIL_WEIGHTS[distance]
        summed = summed + weight * (
            padded[
                4 + distance : 4 + distance + depth_cells, 4 : 4 + cross_cells, 4 : 4 + along_cells
            ]
            + padded[
                4 - distance : 4 - distance + depth_cells, 4 : 4 + cross_cells, 4 : 4 + along_cells
            ]
        )
        summed = summed + weight * (
            padded[
                4 : 4 + depth_cells, 4 + distance : 4 + distance + cross_cells, 4 : 4 + along_cells
            ]
            + padded[
                4 : 4 + depth_cells, 4 - distance : 4 - distance + cross_cells, 4 : 4 + along_cells
            ]
        )
        summed = summed + weight * (
            padded[
                4 : 4 + depth_cells, 4 : 4 + cross_cells, 4 + distance : 4 + distance + along_cells
            ]
            + padded[
                4 : 4 + depth_cells, 4 : 4 + cross_cells, 4 - distance : 4 - distance + along_cells
            ]
        )
    return summed


def aperture_step(
    aperture_speed, wave_zero, wave_one, adjoint_four, adjoint_three, wavelet_pair, position
):
    courant = jnp.square(aperture_speed * STEP_RATIO)
    shape_full = wave_zero.shape
    depth_hit = lax.broadcasted_iota(jnp.int32, shape_full, 0) == position[0]
    cross_hit = lax.broadcasted_iota(jnp.int32, shape_full, 1) == position[1]
    along_hit = lax.broadcasted_iota(jnp.int32, shape_full, 2) == position[2]
    source_mask = jnp.where(depth_hit & cross_hit & along_hit, jnp.float32(1.0), jnp.float32(0.0))
    laplace_zero = laplace(wave_zero)
    laplace_one = laplace(wave_one)
    wave_two = 2.0 * wave_one - wave_zero + courant * laplace_one + wavelet_pair[0] * source_mask
    laplace_two = laplace(wave_two)
    wave_three = 2.0 * wave_two - wave_one + courant * laplace_two + wavelet_pair[1] * source_mask
    laplace_three = laplace(wave_three)
    adjoint_two = 2.0 * adjoint_three - adjoint_four + laplace(courant * adjoint_three)
    adjoint_one = 2.0 * adjoint_two - adjoint_three + laplace(courant * adjoint_two)
    grad_courant = (
        adjoint_one * laplace_zero
        + adjoint_two * laplace_one
        + adjoint_three * laplace_two
        + adjoint_four * laplace_three
    )
    return (wave_three, adjoint_one, grad_courant)


def shards(
    velocity,
    wave_prev,
    wave_now,
    adjoint_next,
    adjoint_now,
    wavelet,
    source_pos,
    cover_start,
    lateral_anchor,
):
    owners = lax.axis_size("dev")
    device = lax.axis_index("dev")
    first_slab = cover_start[device]
    anchor_cross = lateral_anchor[device, 0]
    anchor_along = lateral_anchor[device, 1]
    pieces = []
    for offset in range(-(K - 1), K):
        arrived_slab = velocity if offset == 0 else passed_along(velocity, "dev", -offset)
        arrived = lax.dynamic_slice(arrived_slab, (0, anchor_cross, anchor_along), (SLAB, AX, AY))
        pieces.append(arrived)
    stacked = jnp.stack(pieces, 0)
    start_index = first_slab - device + (K - 1)
    aperture_speed = lax.dynamic_slice_in_dim(stacked, start_index, K, 0).reshape(AZ, AX, AY)
    wave_three, adjoint_one, grad_courant = aperture_step(
        aperture_speed, wave_prev, wave_now, adjoint_next, adjoint_now, wavelet[0], source_pos[0]
    )
    grad_blocks = grad_courant.reshape(K, SLAB, AX, AY)
    padding = jnp.zeros((K - 1, SLAB, AX, AY), jnp.float32)
    padded_blocks = jnp.concatenate([padding, grad_blocks, padding], 0)
    collected = jnp.zeros((SLAB, MX, MY), jnp.float32)
    for offset in range(-(K - 1), K):
        grad_piece = lax.dynamic_index_in_dim(
            padded_blocks, device + offset - first_slab + (K - 1), 0, keepdims=False
        )
        if offset != 0:
            grad_piece = passed_along(grad_piece, "dev", offset)
        sender = jnp.clip(device - offset, 0, owners - 1)
        sender_cross = lateral_anchor[sender, 0]
        sender_along = lateral_anchor[sender, 1]
        region = lax.dynamic_slice(collected, (0, sender_cross, sender_along), (SLAB, AX, AY))
        collected = lax.dynamic_update_slice(
            collected, region + grad_piece, (0, sender_cross, sender_along)
        )
    speed_grad = 2.0 * STEP_RATIO * STEP_RATIO * velocity * collected
    peak_value = lax.pmax(jnp.max(jnp.abs(speed_grad)), "dev")
    gradient = speed_grad / (peak_value + EPSILON)
    return (wave_three, adjoint_one, gradient)


def solution(mesh):
    in_specs = (
        P("dev", None, None),
        P("dev", None, None),
        P("dev", None, None),
        P("dev", None, None),
        P("dev", None, None),
        P("dev", None),
        P("dev", None),
        P(),
        P(),
    )
    out_specs = (P("dev", None, None), P("dev", None, None), P("dev", None, None))
    return jax.shard_map(shards, mesh=mesh, in_specs=in_specs, out_specs=out_specs, check_vma=False)
```

profile of v0, /device:TPU:0, one launch (start us, length us, event | category | flops | bytes accessed | tf_op | source)
XLA Modules:
  0.0 183.8 jit_solution(14309468616336490669)
XLA Ops:
  0.6 4.3 %collective-permute-start = (f32[8,64,256]{2,1,0:T(8,128)}, f32[8,64,256]{2,1,0:T(8,128)S(1)}, u32[]{:S(2)}, u32[]{:S(2)}) collective-permute-start(f32[8,64,256]{2,1,0:T(8,128)} %param.9), channel_id=1, source_target_pairs={{0,3},{1,4},{2,5},{3,6},{4,7},{5,8},{6,9},{7,10},{8,11},{9,12},{10... | collective-permute-start | bytes 1572872 | tf_op jit(solution)/shard_map/ppermute | solution.py:23
  5.0 3.4 %collective-permute-start.1 = (f32[8,64,256]{2,1,0:T(8,128)}, f32[8,64,256]{2,1,0:T(8,128)S(1)}, u32[]{:S(2)}, u32[]{:S(2)}) collective-permute-start(f32[8,64,256]{2,1,0:T(8,128)} %param.9), channel_id=1, source_target_pairs={{0,2},{1,3},{2,4},{3,5},{4,6},{5,7},{6,8},{7,9},{8,10},{9,11},{10,... | collective-permute-start | bytes 1572872 | tf_op jit(solution)/shard_map/ppermute | solution.py:23
  8.4 2.3 %collective-permute-start.2 = (f32[8,64,256]{2,1,0:T(8,128)}, f32[8,64,256]{2,1,0:T(8,128)S(1)}, u32[]{:S(2)}, u32[]{:S(2)}) collective-permute-start(f32[8,64,256]{2,1,0:T(8,128)} %param.9), channel_id=1, source_target_pairs={{0,1},{1,2},{2,3},{3,4},{4,5},{5,6},{6,7},{7,8},{8,9},{9,10},{10,1... | collective-permute-start | bytes 1572872 | tf_op jit(solution)/shard_map/ppermute | solution.py:23
  10.7 1.3 collective-permute-start.3
  12.0 1.3 collective-permute-start.4
  13.3 1.3 dynamic_slice.124
  19.1 2.0 %constant_dynamic-slice_fusion.8 = (s32[1,1]{0,1:T(1,128)}, s32[1,1]{0,1:T(1,128)}, s32[1,1]{0,1:T(1,128)}, s32[1,1]{0,1:T(1,128)}, s32[1,1]{0,1:T(1,128)}, /*in...) fusion(s32[32,2]{0,1:T(2,128)} %param.17, ...), kind=kLoop, calls=%fused_computation.410 | loop fusion | bytes 160 | tf_op jit(solution)/shard_map/dynamic_slice | solution.py:124
  25.1 1.4 fusion.232
  26.4 1.3 iota_compare_fusion.1
  27.8 1.3 fusion.231
  29.1 0.6 iota_compare_fusion
  29.7 0.0 collective-permute-done
  29.7 1.3 collective-permute-start.5
  31.0 0.1 bitcast_dynamic-update-slice_fusion.6
  31.1 0.0 copy-start
  31.1 0.0 copy-start.1
  31.1 0.0 copy-start.3
  31.1 13.5 %collective-permute-done.1 = f32[8,64,256]{2,1,0:T(8,128)S(1)} collective-permute-done((f32[8,64,256]{2,1,0:T(8,128)}, f32[8,64,256]{2,1,0:T(8,128)S(1)}, u32[]{:S(2)}, u32[]{:S(2)}) %collective-permute-start.1) | collective-permute-done | bytes 524320 | tf_op jit(solution)/shard_map/ppermute | solution.py:23
  44.6 0.1 bitcast_dynamic-update-slice_fusion.5
  44.8 0.0 collective-permute-done.2
  44.8 0.1 bitcast_dynamic-update-slice_fusion.4
  44.9 1.1 bitcast_dynamic-update-slice_fusion.3
  46.0 0.0 collective-permute-done.3
  46.0 0.1 bitcast_dynamic-update-slice_fusion.2
  46.1 3.9 %collective-permute-done.4 = f32[8,64,256]{2,1,0:T(8,128)S(1)} collective-permute-done((f32[8,64,256]{2,1,0:T(8,128)}, f32[8,64,256]{2,1,0:T(8,128)S(1)}, u32[]{:S(2)}, u32[]{:S(2)}) %collective-permute-start.4) | collective-permute-done | bytes 524320 | tf_op jit(solution)/shard_map/ppermute | solution.py:23
  50.0 0.1 bitcast_dynamic-update-slice_fusion.1
  50.1 3.1 %collective-permute-done.5 = f32[8,64,256]{2,1,0:T(8,128)S(1)} collective-permute-done((f32[8,64,256]{2,1,0:T(8,128)}, f32[8,64,256]{2,1,0:T(8,128)S(1)}, u32[]{:S(2)}, u32[]{:S(2)}) %collective-permute-start.5) | collective-permute-done | bytes 524320 | tf_op jit(solution)/shard_map/ppermute | solution.py:23
  53.1 0.1 bitcast_dynamic-update-slice_fusion
  53.2 0.1 multiply_multiply_fusion.1
  53.3 0.0 copy-start.4
  53.4 2.6 %fusion = (f32[32,32,128]{2,1,0:T(8,128)S(1)}, f32[32,32,128]{2,1,0:T(8,128)S(1)}, f32[32,32,128]{2,1,0:T(8,128)S(1)}) fusion(f32[4,8,32,128]{3,2,1,0:T(8,128)S(1)} %multiply_multiply_fusion.1, f32[32,32,128]{2,1,0:T(8,128)S(1)} %copy-done, f32[32,32,128]{2,1,0:T(8,128)S(1)} %copy-done.3, f32[]{:T(128)} %bitcast.11, pred[128]{0:T(512)(128)(4,1)S(1)} %iota_compare_fusion, ...), kind=kLoop, calls=%fused_computation.147 | loop fusion | flops 6160384 | bytes 3670212 | tf_op jit(solution)/shard_map/add | solution.py:70
  56.0 4.8 %bitcast_multiply_fusion = (f32[32,32,128]{2,1,0:T(8,128)S(1)}, f32[32,32,128]{2,1,0:T(8,128)S(1)}, f32[32,32,128]{2,1,0:T(8,128)S(1)}, f32[32,32,128]{2,1,0:T(8,128)S(1)}) fusion(f32[4,8,32,128]{3,2,1,0:T(8,128)S(1)} %multiply_multiply_fusion.1, f32[32,32,128]{2,1,0:T(8,128)S(1)} %get-tuple-element.19, f32[32,32,128]{2,1,0:T(8,128)S(1)} %copy-done.4, ...), kind=kLoop, calls=%fused_computation.372 | loop fusion | flops 12189696 | bytes 6291656 | tf_op jit(solution)/shard_map/mul | solution.py:75
  60.8 0.0 copy-start.5
  60.8 5.3 %fusion.165 = (f32[32,32,128]{2,1,0:T(8,128)S(1)}, f32[32,32,128]{2,1,0:T(8,128)}) fusion(f32[32,32,128]{2,1,0:T(8,128)S(1)} %copy-done, f32[32,32,128]{2,1,0:T(8,128)S(1)} %copy-done.4, f32[32,32,128]{2,1,0:T(8,128)S(1)} %get-tuple-element.17, f32[32,32,128]{2,1,0:T(8,128)S(1)} %copy-done.1, f32[32,32,128]{2,1,0:T(8,128)S(1)} %get-tuple-element.18, ...), kind=kLoop, calls=%fused_computation.312 | loop fusion | flops 15859712 | bytes 5242880 | tf_op jit(solution)/shard_map/add | solution.py:77
  66.2 0.1 pad_maximum_fusion
  66.4 0.1 dynamic-slice_bitcast_fusion
  66.5 1.3 collective-permute-start.6
  67.8 1.3 collective-permute-start.7
  96.2 1.3 collective-permute-start.8
  97.5 3.0 %collective-permute-start.9 = (f32[8,32,128]{2,1,0:T(8,128)S(1)}, f32[8,32,128]{2,1,0:T(8,128)S(1)}, u32[]{:S(2)}, u32[]{:S(2)}) collective-permute-start(f32[8,32,128]{2,1,0:T(8,128)S(1)} %get-tuple-element.13), channel_id=1, source_target_pairs={{0,1},{1,2},{2,3},{3,4},{4,5},{5,6},{6,7},{7,8},{8,9},{9,10},{10,1... | collective-permute-start | bytes 393224 | tf_op jit(solution)/shard_map/ppermute | solution.py:23
  100.5 9.6 %collective-permute-start.10 = (f32[8,32,128]{2,1,0:T(8,128)S(1)}, f32[8,32,128]{2,1,0:T(8,128)S(1)}, u32[]{:S(2)}, u32[]{:S(2)}) collective-permute-start(f32[8,32,128]{2,1,0:T(8,128)S(1)} %get-tuple-element.12), channel_id=1, source_target_pairs={{0,2},{1,3},{2,4},{3,5},{4,6},{5,7},{6,8},{7,9},{8,10},{9,11},{10,... | collective-permute-start | bytes 393224 | tf_op jit(solution)/shard_map/ppermute | solution.py:23
  110.1 0.0 collective-permute-done.6
  110.1 5.8 %collective-permute-start.11 = (f32[8,32,128]{2,1,0:T(8,128)S(1)}, f32[8,32,128]{2,1,0:T(8,128)S(1)}, u32[]{:S(2)}, u32[]{:S(2)}) collective-permute-start(f32[8,32,128]{2,1,0:T(8,128)S(1)} %get-tuple-element.11), channel_id=1, source_target_pairs={{0,3},{1,4},{2,5},{3,6},{4,7},{5,8},{6,9},{7,10},{8,11},{9,12},{10... | collective-permute-start | bytes 393224 | tf_op jit(solution)/shard_map/ppermute | solution.py:23
  115.9 3.3 %dynamic_update_slice.21 = f32[8,64,256]{2,1,0:T(8,128)S(1)} dynamic-update-slice(f32[8,64,256]{2,1,0:T(8,128)S(1)} %broadcast_in_dim.16, f32[8,32,128]{2,1,0:T(8,128)S(1)} %collective-permute-done.6, s32[]{:T(128)} %constant.68.clone.1, s32[]{:T(128)S(6)} %select_n.126, s32[]{:T(128)S(6)} %select_n.127) | dynamic-update-slice | bytes 262148 | tf_op jit(solution)/shard_map/dynamic_update_slice | solution.py:126
  119.3 0.0 collective-permute-done.7
  119.3 0.1 dynamic-slice_add_fusion.4
  119.4 3.3 %dynamic_update_slice.22 = f32[8,64,256]{2,1,0:T(8,128)S(1)} dynamic-update-slice(f32[8,64,256]{2,1,0:T(8,128)S(1)} %dynamic_update_slice.21, f32[8,32,128]{2,1,0:T(8,128)S(1)} %dynamic-slice_add_fusion.4, s32[]{:T(128)} %constant.68.clone.1, s32[]{:T(128)S(6)} %select_n.128, s32[]{:T(128)S(6)} %select_n.129) | dynamic-update-slice | bytes 262148 | tf_op jit(solution)/shard_map/dynamic_update_slice | solution.py:126
  122.7 0.1 dynamic-slice_add_fusion.3
  122.9 3.3 %dynamic_update_slice.23 = f32[8,64,256]{2,1,0:T(8,128)S(1)} dynamic-update-slice(f32[8,64,256]{2,1,0:T(8,128)S(1)} %dynamic_update_slice.22, f32[8,32,128]{2,1,0:T(8,128)S(1)} %dynamic-slice_add_fusion.3, s32[]{:T(128)} %constant.68.clone.1, s32[]{:T(128)S(6)} %select_n.131, s32[]{:T(128)S(6)} %select_n.132) | dynamic-update-slice | bytes 262148 | tf_op jit(solution)/shard_map/dynamic_update_slice | solution.py:126
  126.2 0.0 copy-start.2
  126.2 0.1 bitcast_add_fusion
  126.3 1.0 dynamic_update_slice.24
  127.4 0.0 collective-permute-done.9
  127.4 0.1 dynamic-slice_add_fusion.2
  127.5 1.0 dynamic_update_slice.25
  128.5 0.0 collective-permute-done.10
  128.5 0.1 dynamic-slice_add_fusion.1
  128.7 1.0 dynamic_update_slice.26
  129.7 0.0 collective-permute-done.11
  129.7 0.1 dynamic-slice_add_fusion
  129.8 1.0 dynamic_update_slice.27
  130.9 0.7 abs_reduce_fusion
  131.5 50.7 %pmax.7 = f32[]{:T(128)} all-reduce(f32[]{:T(128)} %abs_reduce_fusion), channel_id=1, replica_groups=mesh['dev'=32] {'dev'}, use_global_device_ids=true, to_apply=%region_1.2 | all-reduce | flops 1 | bytes 8 | tf_op jit(solution)/shard_map/pmax | solution.py:130
  182.9 0.9 broadcast_divide_fusion
  (9 shorter events, 0.1 us)
Async XLA Ops:
  0.6 29.1 %collective-permute-start = (f32[8,64,256]{2,1,0:T(8,128)}, f32[8,64,256]{2,1,0:T(8,128)S(1)}, u32[]{:S(2)}, u32[]{:S(2)}) collective-permute-start(f32[8,64,256]{2,1,0:T(8,128)} %param.9), channel_id=1, source_target_pairs={{0,3},{1,4},{2,5},{3,6},{4,7},{5,8},{6,9},{7,10},{8,11},{9,12},{10... | collective-permute-start | bytes 1572872 | tf_op jit(solution)/shard_map/ppermute | solution.py:23
  5.0 39.7 %collective-permute-start.1 = (f32[8,64,256]{2,1,0:T(8,128)}, f32[8,64,256]{2,1,0:T(8,128)S(1)}, u32[]{:S(2)}, u32[]{:S(2)}) collective-permute-start(f32[8,64,256]{2,1,0:T(8,128)} %param.9), channel_id=1, source_target_pairs={{0,2},{1,3},{2,4},{3,5},{4,6},{5,7},{6,8},{7,9},{8,10},{9,11},{10,... | collective-permute-start | bytes 1572872 | tf_op jit(solution)/shard_map/ppermute | solution.py:23
  8.4 36.4 %collective-permute-start.2 = (f32[8,64,256]{2,1,0:T(8,128)}, f32[8,64,256]{2,1,0:T(8,128)S(1)}, u32[]{:S(2)}, u32[]{:S(2)}) collective-permute-start(f32[8,64,256]{2,1,0:T(8,128)} %param.9), channel_id=1, source_target_pairs={{0,1},{1,2},{2,3},{3,4},{4,5},{5,6},{6,7},{7,8},{8,9},{9,10},{10,1... | collective-permute-start | bytes 1572872 | tf_op jit(solution)/shard_map/ppermute | solution.py:23
  10.7 35.2 %collective-permute-start.3 = (f32[8,64,256]{2,1,0:T(8,128)}, f32[8,64,256]{2,1,0:T(8,128)S(1)}, u32[]{:S(2)}, u32[]{:S(2)}) collective-permute-start(f32[8,64,256]{2,1,0:T(8,128)} %param.9), channel_id=1, source_target_pairs={{1,0},{2,1},{3,2},{4,3},{5,4},{6,5},{7,6},{8,7},{9,8},{10,9},{11,1... | collective-permute-start | bytes 1572872 | tf_op jit(solution)/shard_map/ppermute | solution.py:23
  12.0 37.9 %collective-permute-start.4 = (f32[8,64,256]{2,1,0:T(8,128)}, f32[8,64,256]{2,1,0:T(8,128)S(1)}, u32[]{:S(2)}, u32[]{:S(2)}) collective-permute-start(f32[8,64,256]{2,1,0:T(8,128)} %param.9), channel_id=1, source_target_pairs={{2,0},{3,1},{4,2},{5,3},{6,4},{7,5},{8,6},{9,7},{10,8},{11,9},{12,... | collective-permute-start | bytes 1572872 | tf_op jit(solution)/shard_map/ppermute | solution.py:23
  29.7 23.4 %collective-permute-start.5 = (f32[8,64,256]{2,1,0:T(8,128)}, f32[8,64,256]{2,1,0:T(8,128)S(1)}, u32[]{:S(2)}, u32[]{:S(2)}) collective-permute-start(f32[8,64,256]{2,1,0:T(8,128)} %param.9), channel_id=1, source_target_pairs={{3,0},{4,1},{5,2},{6,3},{7,4},{8,5},{9,6},{10,7},{11,8},{12,9},{13... | collective-permute-start | bytes 1572872 | tf_op jit(solution)/shard_map/ppermute | solution.py:23
  31.1 22.2 %copy-start = (f32[32,32,128]{2,1,0:T(8,128)S(1)}, f32[32,32,128]{2,1,0:T(8,128)}, u32[]{:S(2)}) copy-start(f32[32,32,128]{2,1,0:T(8,128)} %param.10) | copy-start | bytes 1572868
  31.1 22.2 %copy-start.1 = (f32[32,32,128]{2,1,0:T(8,128)S(1)}, f32[32,32,128]{2,1,0:T(8,128)}, u32[]{:S(2)}) copy-start(f32[32,32,128]{2,1,0:T(8,128)} %param.13) | copy-start | bytes 1572868
  31.1 22.2 %copy-start.3 = (f32[32,32,128]{2,1,0:T(8,128)S(1)}, f32[32,32,128]{2,1,0:T(8,128)}, u32[]{:S(2)}) copy-start(f32[32,32,128]{2,1,0:T(8,128)} %param.11) | copy-start | bytes 1572868
  53.3 2.6 %copy-start.4 = (f32[32,32,128]{2,1,0:T(8,128)S(1)}, f32[32,32,128]{2,1,0:T(8,128)}, u32[]{:S(2)}) copy-start(f32[32,32,128]{2,1,0:T(8,128)} %param.12) | copy-start | bytes 1572868
  60.8 5.3 %copy-start.5 = (f32[32,32,128]{2,1,0:T(8,128)}, f32[32,32,128]{2,1,0:T(8,128)S(1)}, u32[]{:S(2)}) copy-start(f32[32,32,128]{2,1,0:T(8,128)S(1)} %get-tuple-element.17) | copy-start | bytes 1572868
  66.5 43.6 %collective-permute-start.6 = (f32[8,32,128]{2,1,0:T(8,128)S(1)}, f32[8,32,128]{2,1,0:T(8,128)S(1)}, u32[]{:S(2)}, u32[]{:S(2)}) collective-permute-start(f32[8,32,128]{2,1,0:T(8,128)S(1)} %get-tuple-element.16), channel_id=1, source_target_pairs={{3,0},{4,1},{5,2},{6,3},{7,4},{8,5},{9,6},{10,7},{11,8},{12,9},{13... | collective-permute-start | bytes 393224 | tf_op jit(solution)/shard_map/ppermute | solution.py:23
  67.8 51.5 %collective-permute-start.7 = (f32[8,32,128]{2,1,0:T(8,128)S(1)}, f32[8,32,128]{2,1,0:T(8,128)S(1)}, u32[]{:S(2)}, u32[]{:S(2)}) collective-permute-start(f32[8,32,128]{2,1,0:T(8,128)S(1)} %get-tuple-element.15), channel_id=1, source_target_pairs={{2,0},{3,1},{4,2},{5,3},{6,4},{7,5},{8,6},{9,7},{10,8},{11,9},{12,... | collective-permute-start | bytes 393224 | tf_op jit(solution)/shard_map/ppermute | solution.py:23
  96.2 26.6 %collective-permute-start.8 = (f32[8,32,128]{2,1,0:T(8,128)S(1)}, f32[8,32,128]{2,1,0:T(8,128)S(1)}, u32[]{:S(2)}, u32[]{:S(2)}) collective-permute-start(f32[8,32,128]{2,1,0:T(8,128)S(1)} %get-tuple-element.14), channel_id=1, source_target_pairs={{1,0},{2,1},{3,2},{4,3},{5,4},{6,5},{7,6},{8,7},{9,8},{10,9},{11,1... | collective-permute-start | bytes 393224 | tf_op jit(solution)/shard_map/ppermute | solution.py:23
  97.5 29.9 %collective-permute-start.9 = (f32[8,32,128]{2,1,0:T(8,128)S(1)}, f32[8,32,128]{2,1,0:T(8,128)S(1)}, u32[]{:S(2)}, u32[]{:S(2)}) collective-permute-start(f32[8,32,128]{2,1,0:T(8,128)S(1)} %get-tuple-element.13), channel_id=1, source_target_pairs={{0,1},{1,2},{2,3},{3,4},{4,5},{5,6},{6,7},{7,8},{8,9},{9,10},{10,1... | collective-permute-start | bytes 393224 | tf_op jit(solution)/shard_map/ppermute | solution.py:23
  100.5 28.0 %collective-permute-start.10 = (f32[8,32,128]{2,1,0:T(8,128)S(1)}, f32[8,32,128]{2,1,0:T(8,128)S(1)}, u32[]{:S(2)}, u32[]{:S(2)}) collective-permute-start(f32[8,32,128]{2,1,0:T(8,128)S(1)} %get-tuple-element.12), channel_id=1, source_target_pairs={{0,2},{1,3},{2,4},{3,5},{4,6},{5,7},{6,8},{7,9},{8,10},{9,11},{10,... | collective-permute-start | bytes 393224 | tf_op jit(solution)/shard_map/ppermute | solution.py:23
  110.1 19.6 %collective-permute-start.11 = (f32[8,32,128]{2,1,0:T(8,128)S(1)}, f32[8,32,128]{2,1,0:T(8,128)S(1)}, u32[]{:S(2)}, u32[]{:S(2)}) collective-permute-start(f32[8,32,128]{2,1,0:T(8,128)S(1)} %get-tuple-element.11), channel_id=1, source_target_pairs={{0,3},{1,4},{2,5},{3,6},{4,7},{5,8},{6,9},{7,10},{8,11},{9,12},{10... | collective-permute-start | bytes 393224 | tf_op jit(solution)/shard_map/ppermute | solution.py:23
  126.2 4.6 %copy-start.2 = (f32[8,64,256]{2,1,0:T(8,128)S(1)}, f32[8,64,256]{2,1,0:T(8,128)}, u32[]{:S(2)}) copy-start(f32[8,64,256]{2,1,0:T(8,128)} %param.9) | copy-start | bytes 1572868
where the time goes:
time: 185 us; the launch traced here: 184 us
  blocking collectives  50.7 us (27%)
  between operations  37.3 us (20%)
  starting transfers between devices  36.2 us (20%)
  local copies, waits for them, and re-layouts  22 us (12%)
  waiting for transfers between devices  20.4 us (11%)
  other arithmetic  17.1 us (9%)
    pmax x1, blocking collectives, shards(): peak_value = lax.pmax(jnp.max(jnp.abs(speed_grad)), 'dev')  50.7 us
    ppermute x12, starting transfers between devices, passed_along(): lax.ppermute(value, axis, [(source, source + steps) for source in range(i...  36.2 us
    ppermute x12, waiting for transfers between devices, passed_along(): lax.ppermute(value, axis, [(source, source + steps) for source in range(i...  20.4 us
    dynamic_update_slice x7, local copies, waits for them, and re-layouts, shards(): lax.dynamic_update_slice(collected, region + grad_piece, (0, sender_cross...  14.1 us
    add x1, other arithmetic, aperture_step(): adjoint_one * laplace_zero + adjoint_two * laplace_one  5.32 us
    mul x1, other arithmetic, aperture_step(): courant * adjoint_two  4.83 us
  transfers between devices with their start and end apart: 12, of which 3 were waited for; matrix products, arithmetic and copies ran while one was open for 13% of the time, Pallas kernels for 0%

commit v1 on v0

v1 whole, which is shorter than its diff:
```python
import functools

import jax
import jax.numpy as jnp
from jax import lax
from jax.experimental import pallas as pl
from jax.experimental.pallas import tpu as pltpu
from jax.sharding import PartitionSpec as P

SLAB = 8
K = 4
AX = 32
AY = 128
AZ = 32

WEIGHTS = (-205.0 / 72.0, 8.0 / 5.0, -1.0 / 5.0, 8.0 / 315.0, -1.0 / 560.0)
STEP_RATIO = 0.088
EPSILON = 1e-06
REACH = K - 1
SLOTS = 2 * REACH + 1
OFFSETS = (3, -3, 2, -2, 1, -1)
MESH = pl.DeviceIdType.MESH


def stages_of(count):
    stages, stride = [], 1
    while stride < count:
        left = count // stride
        radix = max(r for r in range(2, max(9, left + 1)) if left % r == 0 and (r <= 8 or r == left))
        if radix > 8:
            radix = next((r for r in range(8, 1, -1) if left % r == 0), left)
        stages.append((stride, radix))
        stride *= radix
    return stages


def kernel(
    n,
    stages,
    vel,
    prev_in,
    now_in,
    adj4_in,
    adj3_in,
    wavelet,
    spos,
    cover,
    anchor,
    wave_out,
    adj_out,
    grad_out,
    pad0,
    pad1,
    pad2,
    pad3,
    padc3,
    padc2,
    q4,
    q3,
    q2,
    lap0,
    lap1,
    lap2,
    cour,
    doubled,
    vsend,
    vrecv,
    gsend,
    grecv,
    total,
    mxsend,
    mxrecv,
    in_sem,
    vs_sem,
    vr_sem,
    gs_sem,
    gr_sem,
    ms_sem,
    mr_sem,
):
    me = lax.axis_index("dev")
    barrier = pltpu.get_barrier_semaphore()
    group = stages[0][1]

    def there(d):
        return (me + d >= 0) & (me + d < n)

    def partner(stride, radix, j):
        digit = (me // stride) % radix
        return me + ((digit + j) % radix - digit) * stride

    expected = 0
    for stride, radix in stages:
        for j in range(1, radix):
            pl.semaphore_signal(
                barrier, inc=1, device_id=(partner(stride, radix, j),), device_id_type=MESH
            )
            expected += 1
    for d in OFFSETS:
        outside = there(d) & ((me + d + group) // group != (me + group) // group)

        @pl.when(outside)
        def _(d=d):
            pl.semaphore_signal(barrier, inc=1, device_id=(me + d,), device_id_type=MESH)

        expected = expected + jnp.where(outside, 1, 0)

    loads = [
        pltpu.make_async_copy(prev_in, pad0.at[4:36, 8:40], in_sem.at[0]),
        pltpu.make_async_copy(now_in, pad1.at[4:36, 8:40], in_sem.at[1]),
        pltpu.make_async_copy(adj4_in, q4, in_sem.at[2]),
        pltpu.make_async_copy(adj3_in, q3, in_sem.at[3]),
    ]
    for load in loads:
        load.start()

    rows = lax.broadcasted_iota(jnp.int32, (AX, AY), 0)
    lanes = lax.broadcasted_iota(jnp.int32, (AX, AY), 1)

    def fold(target):
        cross, along = anchor[target, 0], anchor[target, 1]
        low_lane = lanes >= along
        low_row = rows >= cross
        top = jnp.where(low_lane, vel[:, 0:AX, 0:AY], vel[:, 0:AX, AY : 2 * AY])
        bottom = jnp.where(low_lane, vel[:, AX : 2 * AX, 0:AY], vel[:, AX : 2 * AX, AY : 2 * AY])
        return jnp.where(low_row, top, bottom)

    for d in OFFSETS:
        vsend[d + REACH] = fold(jnp.clip(me + d, 0, n - 1))
    vrecv[REACH] = fold(me)

    pl.semaphore_wait(barrier, expected)

    def v_copy(d):
        return pltpu.make_async_remote_copy(
            src_ref=vsend.at[d + REACH],
            dst_ref=vrecv.at[REACH - d],
            send_sem=vs_sem.at[d + REACH],
            recv_sem=vr_sem.at[REACH - d],
            device_id=(me + d,),
            device_id_type=MESH,
        )

    def g_copy(d):
        return pltpu.make_async_remote_copy(
            src_ref=gsend.at[d + REACH],
            dst_ref=grecv.at[REACH - d],
            send_sem=gs_sem.at[d + REACH],
            recv_sem=gr_sem.at[REACH - d],
            device_id=(me + d,),
            device_id_type=MESH,
        )

    for d in OFFSETS:

        @pl.when(there(d))
        def _(d=d):
            v_copy(d).start()

    for ref in (pad0, pad1, pad2, pad3, padc3, padc2):
        side = jnp.zeros((4, 48, AY), jnp.float32)
        ref[0:4] = side
        ref[36:40] = side

    def clear(z, _):
        edge = jnp.zeros((8, AY), jnp.float32)
        for ref in (pad0, pad1, pad2, pad3, padc3, padc2):
            ref[z + 4, 0:8, :] = edge
            ref[z + 4, 40:48, :] = edge
        return 0

    lax.fori_loop(0, AZ, clear, 0)

    lane_row = lax.broadcasted_iota(jnp.int32, (8, AY), 1)
    ups = [jnp.where(lane_row >= k, jnp.float32(WEIGHTS[k]), 0.0) for k in range(1, 5)]
    downs = [jnp.where(lane_row < AY - k, jnp.float32(WEIGHTS[k]), 0.0) for k in range(1, 5)]

    def lap(ref, z):
        parts = []
        for r in range(8, 40, 8):
            centre = ref[z + 4, r : r + 8, :]
            summed = jnp.float32(3.0 * WEIGHTS[0]) * centre
            for k in range(1, 5):
                summed = summed + jnp.float32(WEIGHTS[k]) * (
                    (ref[z + 4 + k, r : r + 8, :] + ref[z + 4 - k, r : r + 8, :])
                    + (ref[z + 4, r + k : r + k + 8, :] + ref[z + 4, r - k : r - k + 8, :])
                )
                summed = summed + (
                    pltpu.roll(centre, k, 1) * ups[k - 1]
                    + pltpu.roll(centre, AY - k, 1) * downs[k - 1]
                )
            parts.append(summed)
        return jnp.concatenate(parts, 0)

    for load in loads:
        load.wait()

    def first(z, _):
        lap0[z] = lap(pad0, z)
        lap1[z] = lap(pad1, z)
        return 0

    lax.fori_loop(0, AZ, first, 0)

    my_cross, my_along = anchor[me, 0], anchor[me, 1]
    lag = jnp.clip(me - cover[me], 0, K - 1)
    back = lax.rem(AY - my_along, AY)
    ahead = lax.rem(my_along, AY)

    for d in OFFSETS:

        @pl.when(there(d))
        def _(d=d):
            v_copy(-d).wait_recv()

    for k in range(K):
        piece = vrecv[REACH - lag + k]
        speed = pltpu.roll(piece.reshape(SLAB * AX, AY), back, 1) * jnp.float32(STEP_RATIO)
        speed = (speed * speed).reshape(SLAB, AX, AY)
        doubled[SLAB * k : SLAB * (k + 1), 0:AX, :] = speed
        doubled[SLAB * k : SLAB * (k + 1), AX : 2 * AX, :] = speed

    plane_hit = (rows == spos[0, 1]) & (lanes == spos[0, 2])
    plane_one = jnp.where(plane_hit, wavelet[0, 0], 0.0)
    plane_two = jnp.where(plane_hit, wavelet[0, 1], 0.0)
    source_depth = spos[0, 0]

    def second(z, _):
        c = doubled[z, pl.ds(my_cross, AX), :]
        cour[z] = c
        hit = jnp.where(source_depth == z, jnp.float32(1.0), jnp.float32(0.0))
        pad2[z + 4, 8:40, :] = (
            2.0 * pad1[z + 4, 8:40, :] - pad0[z + 4, 8:40, :] + c * lap1[z] + hit * plane_one
        )
        padc3[z + 4, 8:40, :] = c * q3[z]
        return 0

    lax.fori_loop(0, AZ, second, 0)

    def third(z, _):
        c = cour[z]
        hit = jnp.where(source_depth == z, jnp.float32(1.0), jnp.float32(0.0))
        two = lap(pad2, z)
        lap2[z] = two
        p3 = 2.0 * pad2[z + 4, 8:40, :] - pad1[z + 4, 8:40, :] + c * two + hit * plane_two
        pad3[z + 4, 8:40, :] = p3
        wave_out[z] = p3
        a2 = 2.0 * q3[z] - q4[z] + lap(padc3, z)
        q2[z] = a2
        padc2[z + 4, 8:40, :] = c * a2
        return 0

    lax.fori_loop(0, AZ, third, 0)

    def fourth(z, _):
        q1 = 2.0 * q2[z] - q3[z] + lap(padc2, z)
        adj_out[z] = q1
        g = q1 * lap0[z] + q2[z] * lap1[z] + q3[z] * lap2[z] + q4[z] * lap(pad3, z)
        g = pltpu.roll(g, ahead, 1)
        doubled[z, 0:AX, :] = g
        doubled[z, AX : 2 * AX, :] = g
        return 0

    lax.fori_loop(0, AZ, fourth, 0)

    def rolled(d):
        index = jnp.clip(d + lag, 0, K - 1)
        return doubled[pl.ds(index * SLAB, SLAB), pl.ds(AX - my_cross, AX), :]

    for d in OFFSETS:
        gsend[d + REACH] = rolled(d)

        @pl.when(there(d))
        def _(d=d):
            g_copy(d).start()

    grecv[REACH] = rolled(0)
    total[...] = jnp.zeros_like(total)

    def add_piece(offset):
        sender = jnp.clip(me + offset, 0, n - 1)
        cross, along = anchor[sender, 0], anchor[sender, 1]
        gap = me - cover[sender]
        covered = jnp.where((gap >= 0) & (gap < K), 1, 0)
        for i in range(2):
            for j in range(2):
                row_ok = rows >= cross if i == 0 else rows < cross
                lane_ok = lanes >= along if j == 0 else lanes < along
                ok = row_ok & lane_ok & (covered + jnp.zeros_like(rows) > 0)
                view = total.at[:, AX * i : AX * (i + 1), AY * j : AY * (j + 1)]
                view[...] = view[...] + jnp.where(ok, grecv[offset + REACH], 0.0)

    add_piece(0)
    for d in (1, -1, 2, -2, 3, -3):

        @pl.when(there(d))
        def _(d=d):
            g_copy(-d).wait_recv()
            add_piece(d)

    largest = jnp.zeros((8, AY), jnp.float32)
    for z in range(SLAB):
        sg = jnp.float32(2.0 * STEP_RATIO * STEP_RATIO) * vel[z] * total[z]
        total[z] = sg
        mag = jnp.abs(sg)
        mag = jnp.maximum(mag[:, 0:AY], mag[:, AY : 2 * AY])
        mag = mag.reshape(8, 8, AY).max(0)
        largest = jnp.maximum(largest, mag)

    base = 0
    waits = []
    for index, (stride, radix) in enumerate(stages):
        mxsend[index] = largest
        copies = []
        for j in range(1, radix):
            copies.append(
                pltpu.make_async_remote_copy(
                    src_ref=mxsend.at[index],
                    dst_ref=mxrecv.at[base + j - 1],
                    send_sem=ms_sem.at[base + j - 1],
                    recv_sem=mr_sem.at[base + j - 1],
                    device_id=(partner(stride, radix, j),),
                    device_id_type=MESH,
                )
            )
        for copy in copies:
            copy.start()
        for j, copy in enumerate(copies):
            copy.wait_recv()
            largest = jnp.maximum(largest, mxrecv[base + j])
        waits += copies
        base += radix - 1

    peak = jnp.max(largest) + jnp.float32(EPSILON)
    for z in range(SLAB):
        grad_out[z] = total[z] / peak

    for d in OFFSETS:

        @pl.when(there(d))
        def _(d=d):
            v_copy(d).wait_send()
            g_copy(d).wait_send()

    for copy in waits:
        copy.wait_send()


def shards(n, vel, prev, now, adj4, adj3, wavelet, spos, cover, anchor):
    stages = stages_of(n)
    partners = sum(radix - 1 for _, radix in stages)
    f32 = jnp.float32
    any_spec = pl.BlockSpec(memory_space=pl.ANY)
    vmem = pl.BlockSpec(memory_space=pltpu.VMEM)
    smem = pl.BlockSpec(memory_space=pltpu.SMEM)
    field = pltpu.VMEM((AZ, AX, AY), f32)
    padded = pltpu.VMEM((AZ + 8, AX + 16, AY), f32)
    pieces = pltpu.VMEM((SLOTS, SLAB, AX, AY), f32)
    dma = pltpu.SemaphoreType.DMA
    return pl.pallas_call(
        functools.partial(kernel, n, stages),
        out_shape=(
            jax.ShapeDtypeStruct((AZ, AX, AY), f32),
            jax.ShapeDtypeStruct((AZ, AX, AY), f32),
            jax.ShapeDtypeStruct(vel.shape, f32),
        ),
        in_specs=[vmem] + [any_spec] * 4 + [smem] * 4,
        out_specs=(vmem, vmem, vmem),
        scratch_shapes=[padded] * 6
        + [field] * 7
        + [pltpu.VMEM((AZ, 2 * AX, AY), f32)]
        + [pieces] * 4
        + [
            pltpu.VMEM(vel.shape, f32),
            pltpu.VMEM((len(stages), 8, AY), f32),
            pltpu.VMEM((partners, 8, AY), f32),
            dma((4,)),
            dma((SLOTS,)),
            dma((SLOTS,)),
            dma((SLOTS,)),
            dma((SLOTS,)),
            dma((partners,)),
            dma((partners,)),
        ],
        compiler_params=pltpu.CompilerParams(
            collective_id=0, has_side_effects=True, vmem_limit_bytes=48 * 1024 * 1024
        ),
    )(vel, prev, now, adj4, adj3, wavelet, spos, cover, anchor)


def solution(mesh):
    cube, pair = P("dev", None, None), P("dev", None)
    return jax.shard_map(
        functools.partial(shards, mesh.shape["dev"]),
        mesh=mesh,
        in_specs=(cube, cube, cube, cube, cube, pair, pair, P(), P()),
        out_specs=(cube, cube, cube),
        check_vma=False,
    )
```

time: 185 us -> 60.4 us (0.33)
  Pallas kernels: 0 us -> 50.9 us
  blocking collectives: 50.7 us -> 0 us
  between operations: 37.3 us -> 0.69 us
  starting transfers between devices: 36.2 us -> 0 us
  waiting for transfers between devices: 20.4 us -> 0 us
  other arithmetic: 17.1 us -> 0 us
  local copies, waits for them, and re-layouts: 22 us -> 8.37 us
    pallas_call x0 -> x1, Pallas kernels: none -> 50.9 us  [shards(): pl.pallas_call(functools.partial(kernel, n, stages), out_shape=(jax.Shape...]
    pmax x1 -> x0, blocking collectives: 50.7 us -> none  [shards(): peak_value = lax.pmax(jnp.max(jnp.abs(speed_grad)), 'dev')]
    ppermute x12 -> x0, starting transfers between devices: 36.2 us -> none  [passed_along(): lax.ppermute(value, axis, [(source, source + steps) for source in range(i...]
    ppermute x12 -> x0, waiting for transfers between devices: 20.4 us -> none  [passed_along(): lax.ppermute(value, axis, [(source, source + steps) for source in range(i...]
    dynamic_update_slice x7 -> x0, local copies, waits for them, and re-layouts: 14.1 us -> none  [shards(): lax.dynamic_update_slice(collected, region + grad_piece, (0, sender_cross...]
    add x8 -> x0, other arithmetic: 8.62 us -> none  [the longest x1 5.32 us: aperture_step(): adjoint_one * laplace_zero + adjoint_two * laplace_one]
    unnamed x18 -> x20, local copies, waits for them, and re-layouts: 1.66 us -> 8.37 us
    mul x1 -> x0, other arithmetic: 4.83 us -> none  [aperture_step(): courant * adjoint_two]
  transfers between devices with their start and end apart: 12 -> 0, of which waited for: 3 -> 0; matrix products, arithmetic and copies ran while one was open for 13% -> 0% of each run, Pallas kernels for 0% -> 0%
where the time goes in v1:
time: 60.4 us; the launch traced here: 60 us
  Pallas kernels  50.9 us (84%)
  local copies, waits for them, and re-layouts  8.37 us (14%)
  between operations  0.69 us (1%)
    pallas_call x1, Pallas kernels, shards(): pl.pallas_call(functools.partial(kernel, n, stages), out_shape=(jax.Shape...  50.9 us
    unnamed x20, local copies, waits for them, and re-layouts  8.37 us

profile of v1, /device:TPU:0, one launch (start us, length us, event | category | flops | bytes accessed | tf_op | source)
XLA Modules:
  0.0 60.0 jit_solution(13699122908647226758)
XLA Ops:
  0.6 0.0 copy-start.7
  0.6 0.0 copy-start.6
  0.7 0.0 copy-start.5
  0.7 0.8 %copy.12.anchor = s32[32,2]{1,0:T(8,128)S(1)} copy(s32[32,2]{0,1:T(2,128)} %param.17) | data formatting | bytes 512 | tf_op args[8]
  1.4 0.0 copy-done.7
  1.4 0.0 copy-done.6
  1.4 0.0 copy-done.5
  1.5 0.0 copy-start
  1.5 1.0 %copy-done = f32[8,64,256]{2,1,0:T(8,128)S(1)} copy-done((f32[8,64,256]{2,1,0:T(8,128)S(1)}, f32[8,64,256]{2,1,0:T(8,128)}, u32[]{:S(2)}) %copy-start) | copy-done | bytes 524312
  2.5 0.0 copy-start.1
  2.5 1.0 %copy-done.1 = f32[32,32,128]{2,1,0:T(8,128)S(1)} copy-done((f32[32,32,128]{2,1,0:T(8,128)S(1)}, f32[32,32,128]{2,1,0:T(8,128)}, u32[]{:S(2)}) %copy-start.1) | copy-done | bytes 524312
  3.5 0.0 copy-start.2
  3.5 1.0 %copy-done.2 = f32[32,32,128]{2,1,0:T(8,128)S(1)} copy-done((f32[32,32,128]{2,1,0:T(8,128)S(1)}, f32[32,32,128]{2,1,0:T(8,128)}, u32[]{:S(2)}) %copy-start.2) | copy-done | bytes 524312
  4.6 0.0 copy-start.3
  4.6 1.0 %copy-done.3 = f32[32,32,128]{2,1,0:T(8,128)S(1)} copy-done((f32[32,32,128]{2,1,0:T(8,128)S(1)}, f32[32,32,128]{2,1,0:T(8,128)}, u32[]{:S(2)}) %copy-start.3) | copy-done | bytes 524312
  5.6 0.0 copy-start.4
  5.6 1.0 %copy-done.4 = f32[32,32,128]{2,1,0:T(8,128)S(1)} copy-done((f32[32,32,128]{2,1,0:T(8,128)S(1)}, f32[32,32,128]{2,1,0:T(8,128)}, u32[]{:S(2)}) %copy-start.4) | copy-done | bytes 524312
  6.7 50.9 %shard_map.112 = (f32[32,32,128]{2,1,0:T(8,128)S(1)}, f32[32,32,128]{2,1,0:T(8,128)S(1)}, f32[8,64,256]{2,1,0:T(8,128)S(1)}) custom-call(f32[8,64,256]{2,1,0:T(8,128)S(1)} %copy-done, f32[32,32,128]{2,1,0:T(8,128)S(1)} %copy-done.1, f32[32,32,128]{2,1,0:T(8,128)S(1)} %copy-done.2, f32[32,32,128]{2,1,0:T(8,128)S(1)} %copy-done.3, ...), custom_call_target="tpu_custom_call" | custom-call | tf_op jit(solution)/shard_map/pallas_call | solution.py:360
  57.6 0.8 %copy.16 = f32[32,32,128]{2,1,0:T(8,128)} copy(f32[32,32,128]{2,1,0:T(8,128)S(1)} %get-tuple-element.6) | data formatting | bytes 1048576
  58.4 0.8 %copy.17 = f32[32,32,128]{2,1,0:T(8,128)} copy(f32[32,32,128]{2,1,0:T(8,128)S(1)} %get-tuple-element.7) | data formatting | bytes 1048576
  59.2 0.8 %copy.18 = f32[8,64,256]{2,1,0:T(8,128)} copy(f32[8,64,256]{2,1,0:T(8,128)S(1)} %get-tuple-element.8) | data formatting | bytes 1048576
Async XLA Ops:
  0.6 0.8 %copy-start.7 = (s32[32]{0:T(128)S(1)}, s32[32]{0:T(128)}, u32[]{:S(2)}) copy-start(s32[32]{0:T(128)} %cover.1) | copy-start | bytes 388
  0.6 0.8 %copy-start.6 = (s32[1,3]{1,0:T(1,128)S(1)}, s32[1,3]{1,0:T(1,128)}, u32[]{:S(2)}) copy-start(s32[1,3]{1,0:T(1,128)} %spos.1) | copy-start | bytes 40
  0.7 0.8 %copy-start.5 = (f32[1,2]{1,0:T(1,128)S(1)}, f32[1,2]{1,0:T(1,128)}, u32[]{:S(2)}) copy-start(f32[1,2]{1,0:T(1,128)} %wavelet.1) | copy-start | bytes 28
  1.5 1.0 %copy-start = (f32[8,64,256]{2,1,0:T(8,128)S(1)}, f32[8,64,256]{2,1,0:T(8,128)}, u32[]{:S(2)}) copy-start(f32[8,64,256]{2,1,0:T(8,128)} %vel.1) | copy-start | bytes 1572868
  2.5 1.0 %copy-start.1 = (f32[32,32,128]{2,1,0:T(8,128)S(1)}, f32[32,32,128]{2,1,0:T(8,128)}, u32[]{:S(2)}) copy-start(f32[32,32,128]{2,1,0:T(8,128)} %prev_in.1) | copy-start | bytes 1572868
  3.5 1.0 %copy-start.2 = (f32[32,32,128]{2,1,0:T(8,128)S(1)}, f32[32,32,128]{2,1,0:T(8,128)}, u32[]{:S(2)}) copy-start(f32[32,32,128]{2,1,0:T(8,128)} %now_in.1) | copy-start | bytes 1572868
  4.6 1.0 %copy-start.3 = (f32[32,32,128]{2,1,0:T(8,128)S(1)}, f32[32,32,128]{2,1,0:T(8,128)}, u32[]{:S(2)}) copy-start(f32[32,32,128]{2,1,0:T(8,128)} %adj4_in.1) | copy-start | bytes 1572868
  5.6 1.0 %copy-start.4 = (f32[32,32,128]{2,1,0:T(8,128)S(1)}, f32[32,32,128]{2,1,0:T(8,128)}, u32[]{:S(2)}) copy-start(f32[32,32,128]{2,1,0:T(8,128)} %adj3_in.1) | copy-start | bytes 1572868

commit v2 on v1

--- a/solution.py
+++ b/solution.py
@@ -17,6 +17,7 @@
 STEP_RATIO = 0.088
 EPSILON = 1e-06
 REACH = K - 1
+HALF = SLAB // 2
 SLOTS = 2 * REACH + 1
 OFFSETS = (3, -3, 2, -2, 1, -1)
 MESH = pl.DeviceIdType.MESH
@@ -37,7 +38,7 @@
 def kernel(
     n,
     stages,
-    vel,
+    vel_in,
     prev_in,
     now_in,
     adj4_in,
@@ -46,9 +47,12 @@
     spos,
     cover,
     anchor,
+    wave_hbm,
+    adj_hbm,
+    grad_out,
+    vel,
     wave_out,
     adj_out,
-    grad_out,
     pad0,
     pad1,
     pad2,
@@ -71,6 +75,7 @@
     mxsend,
     mxrecv,
     in_sem,
+    out_sem,
     vs_sem,
     vr_sem,
     gs_sem,
@@ -79,6 +84,8 @@
     mr_sem,
 ):
     me = lax.axis_index("dev")
+    vel_load = pltpu.make_async_copy(vel_in, vel, in_sem.at[4])
+    vel_load.start()
     barrier = pltpu.get_barrier_semaphore()
     group = stages[0][1]
 
@@ -125,6 +132,7 @@
         bottom = jnp.where(low_lane, vel[:, AX : 2 * AX, 0:AY], vel[:, AX : 2 * AX, AY : 2 * AY])
         return jnp.where(low_row, top, bottom)
 
+    vel_load.wait()
     for d in OFFSETS:
         vsend[d + REACH] = fold(jnp.clip(me + d, 0, n - 1))
     vrecv[REACH] = fold(me)
@@ -141,12 +149,13 @@
             device_id_type=MESH,
         )
 
-    def g_copy(d):
+    def g_copy(d, half):
+        planes = pl.ds(half * HALF, HALF)
         return pltpu.make_async_remote_copy(
-            src_ref=gsend.at[d + REACH],
-            dst_ref=grecv.at[REACH - d],
-            send_sem=gs_sem.at[d + REACH],
-            recv_sem=gr_sem.at[REACH - d],
+            src_ref=gsend.at[d + REACH, planes],
+            dst_ref=grecv.at[REACH - d, planes],
+            send_sem=gs_sem.at[half, d + REACH],
+            recv_sem=gr_sem.at[half, REACH - d],
             device_id=(me + d,),
             device_id_type=MESH,
         )
@@ -169,7 +178,7 @@
             ref[z + 4, 40:48, :] = edge
         return 0
 
-    lax.fori_loop(0, AZ, clear, 0)
+    lax.fori_loop(0, AZ, clear, 0, unroll=2)
 
     lane_row = lax.broadcasted_iota(jnp.int32, (8, AY), 1)
     ups = [jnp.where(lane_row >= k, jnp.float32(WEIGHTS[k]), 0.0) for k in range(1, 5)]
@@ -200,7 +209,7 @@
         lap1[z] = lap(pad1, z)
         return 0
 
-    lax.fori_loop(0, AZ, first, 0)
+    lax.fori_loop(0, AZ, first, 0, unroll=2)
 
     my_cross, my_along = anchor[me, 0], anchor[me, 1]
     lag = jnp.clip(me - cover[me], 0, K - 1)
@@ -235,7 +244,7 @@
         padc3[z + 4, 8:40, :] = c * q3[z]
         return 0
 
-    lax.fori_loop(0, AZ, second, 0)
+    lax.fori_loop(0, AZ, second, 0, unroll=4)
 
     def third(z, _):
         c = cour[z]
@@ -250,31 +259,38 @@
         padc2[z + 4, 8:40, :] = c * a2
         return 0
 
-    lax.fori_loop(0, AZ, third, 0)
-
-    def fourth(z, _):
+    lax.fori_loop(0, AZ, third, 0, unroll=2)
+    wave_store = pltpu.make_async_copy(wave_out, wave_hbm, out_sem.at[0])
+    adj_store = pltpu.make_async_copy(adj_out, adj_hbm, out_sem.at[1])
+    wave_store.start()
+
+    def fourth(step, half):
+        z = (step // HALF) * SLAB + half * HALF + lax.rem(step, HALF)
         q1 = 2.0 * q2[z] - q3[z] + lap(padc2, z)
         adj_out[z] = q1
         g = q1 * lap0[z] + q2[z] * lap1[z] + q3[z] * lap2[z] + q4[z] * lap(pad3, z)
         g = pltpu.roll(g, ahead, 1)
         doubled[z, 0:AX, :] = g
         doubled[z, AX : 2 * AX, :] = g
-        return 0
-
-    lax.fori_loop(0, AZ, fourth, 0)
-
-    def rolled(d):
+        return half
+
+    def rolled(d, half):
         index = jnp.clip(d + lag, 0, K - 1)
-        return doubled[pl.ds(index * SLAB, SLAB), pl.ds(AX - my_cross, AX), :]
-
-    for d in OFFSETS:
-        gsend[d + REACH] = rolled(d)
-
-        @pl.when(there(d))
-        def _(d=d):
-            g_copy(d).start()
-
-    grecv[REACH] = rolled(0)
+        return doubled[pl.ds(index * SLAB + half * HALF, HALF), pl.ds(AX - my_cross, AX), :]
+
+    for half in range(2):
+        planes = slice(half * HALF, (half + 1) * HALF)
+        lax.fori_loop(0, AZ // 2, fourth, half, unroll=2)
+        for d in OFFSETS:
+            gsend[d + REACH, planes] = rolled(d, half)
+
+            @pl.when(there(d))
+            def _(d=d, half=half):
+                g_copy(d, half).start()
+
+        grecv[REACH, planes] = rolled(0, half)
+
+    adj_store.start()
     total[...] = jnp.zeros_like(total)
 
     def add_piece(offset):
@@ -295,7 +311,8 @@
 
         @pl.when(there(d))
         def _(d=d):
-            g_copy(-d).wait_recv()
+            g_copy(-d, 0).wait_recv()
+            g_copy(-d, 1).wait_recv()
             add_piece(d)
 
     largest = jnp.zeros((8, AY), jnp.float32)
@@ -340,8 +357,11 @@
         @pl.when(there(d))
         def _(d=d):
             v_copy(d).wait_send()
-            g_copy(d).wait_send()
-
+            g_copy(d, 0).wait_send()
+            g_copy(d, 1).wait_send()
+
+    wave_store.wait()
+    adj_store.wait()
     for copy in waits:
         copy.wait_send()
 
@@ -350,7 +370,7 @@
     stages = stages_of(n)
     partners = sum(radix - 1 for _, radix in stages)
     f32 = jnp.float32
-    any_spec = pl.BlockSpec(memory_space=pl.ANY)
+    hbm = pl.BlockSpec(memory_space=pltpu.HBM)
     vmem = pl.BlockSpec(memory_space=pltpu.VMEM)
     smem = pl.BlockSpec(memory_space=pltpu.SMEM)
     field = pltpu.VMEM((AZ, AX, AY), f32)
@@ -364,9 +384,10 @@
             jax.ShapeDtypeStruct((AZ, AX, AY), f32),
             jax.ShapeDtypeStruct(vel.shape, f32),
         ),
-        in_specs=[vmem] + [any_spec] * 4 + [smem] * 4,
-        out_specs=(vmem, vmem, vmem),
-        scratch_shapes=[padded] * 6
+        in_specs=[hbm] * 5 + [smem] * 4,
+        out_specs=(hbm, hbm, vmem),
+        scratch_shapes=[pltpu.VMEM(vel.shape, f32), field, field]
+        + [padded] * 6
         + [field] * 7
         + [pltpu.VMEM((AZ, 2 * AX, AY), f32)]
         + [pieces] * 4
@@ -374,16 +395,17 @@
             pltpu.VMEM(vel.shape, f32),
             pltpu.VMEM((len(stages), 8, AY), f32),
             pltpu.VMEM((partners, 8, AY), f32),
-            dma((4,)),
+            dma((5,)),
+            dma((2,)),
             dma((SLOTS,)),
             dma((SLOTS,)),
-            dma((SLOTS,)),
-            dma((SLOTS,)),
+            dma((2, SLOTS)),
+            dma((2, SLOTS)),
             dma((partners,)),
             dma((partners,)),
         ],
         compiler_params=pltpu.CompilerParams(
-            collective_id=0, has_side_effects=True, vmem_limit_bytes=48 * 1024 * 1024
+            collective_id=0, has_side_effects=True, vmem_limit_bytes=60 * 1024 * 1024
         ),
     )(vel, prev, now, adj4, adj3, wavelet, spos, cover, anchor)
 

time: 60.4 us -> 52.9 us (0.88)
  Pallas kernels: 50.9 us -> 46.6 us
  local copies, waits for them, and re-layouts: 8.37 us -> 5.32 us
    pallas_call x1, Pallas kernels: 50.9 us -> 46.6 us  [shards(): pl.pallas_call(functools.partial(kernel, n, stages), out_shape=(jax.Shape...]
    unnamed x20 -> x8, local copies, waits for them, and re-layouts: 8.37 us -> 5.32 us
where the time goes in v2:
time: 52.9 us; the launch traced here: 52.6 us
  Pallas kernels  46.6 us (88%)
  local copies, waits for them, and re-layouts  5.32 us (10%)
  between operations  0.65 us (1%)
    pallas_call x1, Pallas kernels, shards(): pl.pallas_call(functools.partial(kernel, n, stages), out_shape=(jax.Shape...  46.6 us
    unnamed x8, local copies, waits for them, and re-layouts  5.32 us

profile of v2, /device:TPU:0, one launch (start us, length us, event | category | flops | bytes accessed | tf_op | source)
XLA Modules:
  0.0 52.6 jit_solution(9132714322207181358)
XLA Ops:
  0.6 1.4 %copy.12.anchor = s32[32,2]{1,0:T(8,128)} copy(s32[32,2]{0,1:T(2,128)} %param.17) | data formatting | bytes 512 | tf_op args[8]
  2.0 46.6 %shard_map.112 = (f32[32,32,128]{2,1,0:T(8,128)}, f32[32,32,128]{2,1,0:T(8,128)}, f32[8,64,256]{2,1,0:T(8,128)}) custom-call(f32[8,64,256]{2,1,0:T(8,128)} %vel_in.1, f32[32,32,128]{2,1,0:T(8,128)} %prev_in.1, f32[32,32,128]{2,1,0:T(8,128)} %now_in.1, f32[32,32,128]{2,1,0:T(8,128)} %adj4_in.1, f32[32,32,128]{2,1,0:T(8,128)} %adj3_in.1, f32[1,2]{1,0:T(1,128)} %wavelet.1, ...), custom_call_target="tpu_custom_call" | custom-call | tf_op jit(solution)/shard_map/pallas_call | solution.py:380
  48.7 0.0 copy-start.1
  48.7 1.9 %copy.16 = f32[32,32,128]{2,1,0:T(8,128)} copy(f32[32,32,128]{2,1,0:T(8,128)} %get-tuple-element.6) | data formatting | bytes 1048576
  50.6 0.0 copy-done.1
  50.6 0.0 copy-start
  50.6 0.8 %copy.17 = f32[32,32,128]{2,1,0:T(8,128)} copy(f32[32,32,128]{2,1,0:T(8,128)S(1)} %copy-done.1) | data formatting | bytes 1048576
  51.4 0.4 copy-done
  51.8 0.8 %copy.18 = f32[8,64,256]{2,1,0:T(8,128)} copy(f32[8,64,256]{2,1,0:T(8,128)S(1)} %copy-done) | data formatting | bytes 1048576
Async XLA Ops:
  48.7 1.9 %copy-start.1 = (f32[32,32,128]{2,1,0:T(8,128)S(1)}, f32[32,32,128]{2,1,0:T(8,128)}, u32[]{:S(2)}) copy-start(f32[32,32,128]{2,1,0:T(8,128)} %get-tuple-element.7) | copy-start | bytes 1572868
  50.6 1.2 %copy-start = (f32[8,64,256]{2,1,0:T(8,128)S(1)}, f32[8,64,256]{2,1,0:T(8,128)}, u32[]{:S(2)}) copy-start(f32[8,64,256]{2,1,0:T(8,128)} %get-tuple-element.8) | copy-start | bytes 1572868

commit v3 on v2

--- a/solution.py
+++ b/solution.py
@@ -125,7 +125,7 @@
     lanes = lax.broadcasted_iota(jnp.int32, (AX, AY), 1)
 
     def fold(target):
-        cross, along = anchor[target, 0], anchor[target, 1]
+        cross, along = anchor[0, target], anchor[1, target]
         low_lane = lanes >= along
         low_row = rows >= cross
         top = jnp.where(low_lane, vel[:, 0:AX, 0:AY], vel[:, 0:AX, AY : 2 * AY])
@@ -209,9 +209,9 @@
         lap1[z] = lap(pad1, z)
         return 0
 
-    lax.fori_loop(0, AZ, first, 0, unroll=2)
-
-    my_cross, my_along = anchor[me, 0], anchor[me, 1]
+    lax.fori_loop(0, AZ, first, 0, unroll=4)
+
+    my_cross, my_along = anchor[0, me], anchor[1, me]
     lag = jnp.clip(me - cover[me], 0, K - 1)
     back = lax.rem(AY - my_along, AY)
     ahead = lax.rem(my_along, AY)
@@ -259,7 +259,7 @@
         padc2[z + 4, 8:40, :] = c * a2
         return 0
 
-    lax.fori_loop(0, AZ, third, 0, unroll=2)
+    lax.fori_loop(0, AZ, third, 0, unroll=4)
     wave_store = pltpu.make_async_copy(wave_out, wave_hbm, out_sem.at[0])
     adj_store = pltpu.make_async_copy(adj_out, adj_hbm, out_sem.at[1])
     wave_store.start()
@@ -280,7 +280,7 @@
 
     for half in range(2):
         planes = slice(half * HALF, (half + 1) * HALF)
-        lax.fori_loop(0, AZ // 2, fourth, half, unroll=2)
+        lax.fori_loop(0, AZ // 2, fourth, half, unroll=4)
         for d in OFFSETS:
             gsend[d + REACH, planes] = rolled(d, half)
 
@@ -295,7 +295,7 @@
 
     def add_piece(offset):
         sender = jnp.clip(me + offset, 0, n - 1)
-        cross, along = anchor[sender, 0], anchor[sender, 1]
+        cross, along = anchor[0, sender], anchor[1, sender]
         gap = me - cover[sender]
         covered = jnp.where((gap >= 0) & (gap < K), 1, 0)
         for i in range(2):
@@ -407,7 +407,7 @@
         compiler_params=pltpu.CompilerParams(
             collective_id=0, has_side_effects=True, vmem_limit_bytes=60 * 1024 * 1024
         ),
-    )(vel, prev, now, adj4, adj3, wavelet, spos, cover, anchor)
+    )(vel, prev, now, adj4, adj3, wavelet, spos, cover, anchor.T)
 
 
 def solution(mesh):

time: 52.9 us -> 50.5 us (0.955)
  local copies, waits for them, and re-layouts: 5.32 us -> 3.95 us
  Pallas kernels: 46.6 us -> 45.7 us
    unnamed x8 -> x7, local copies, waits for them, and re-layouts: 5.32 us -> 3.95 us
    pallas_call x1, Pallas kernels: 46.6 us -> 45.7 us  [shards(): pl.pallas_call(functools.partial(kernel, n, stages), out_shape=(jax.Shape...]
where the time goes in v3:
time: 50.5 us; the launch traced here: 50.3 us
  Pallas kernels  45.7 us (90%)
  local copies, waits for them, and re-layouts  3.95 us (8%)
  between operations  0.65 us (1%)
    pallas_call x1, Pallas kernels, shards(): pl.pallas_call(functools.partial(kernel, n, stages), out_shape=(jax.Shape...  45.7 us
    unnamed x7, local copies, waits for them, and re-layouts  3.95 us

profile of v3, /device:TPU:0, one launch (start us, length us, event | category | flops | bytes accessed | tf_op | source)
XLA Modules:
  0.0 50.3 jit_solution(2301871900917435078)
XLA Ops:
  0.6 45.7 %shard_map.112 = (f32[32,32,128]{2,1,0:T(8,128)}, f32[32,32,128]{2,1,0:T(8,128)}, f32[8,64,256]{2,1,0:T(8,128)}) custom-call(f32[8,64,256]{2,1,0:T(8,128)} %vel_in.1, f32[32,32,128]{2,1,0:T(8,128)} %prev_in.1, f32[32,32,128]{2,1,0:T(8,128)} %now_in.1, f32[32,32,128]{2,1,0:T(8,128)} %adj4_in.1, f32[32,32,128]{2,1,0:T(8,128)} %adj3_in.1, f32[1,2]{1,0:T(1,128)} %wavelet.1, ...), custom_call_target="tpu_custom_call" | custom-call | tf_op jit(solution)/shard_map/pallas_call | solution.py:380
  46.4 0.0 copy-start.1
  46.4 1.9 %copy.15 = f32[32,32,128]{2,1,0:T(8,128)} copy(f32[32,32,128]{2,1,0:T(8,128)} %get-tuple-element.6) | data formatting | bytes 1048576
  48.3 0.0 copy-done.1
  48.3 0.0 copy-start
  48.3 0.8 %copy.16 = f32[32,32,128]{2,1,0:T(8,128)} copy(f32[32,32,128]{2,1,0:T(8,128)S(1)} %copy-done.1) | data formatting | bytes 1048576
  49.1 0.4 copy-done
  49.5 0.8 %copy.17 = f32[8,64,256]{2,1,0:T(8,128)} copy(f32[8,64,256]{2,1,0:T(8,128)S(1)} %copy-done) | data formatting | bytes 1048576
Async XLA Ops:
  46.4 1.9 %copy-start.1 = (f32[32,32,128]{2,1,0:T(8,128)S(1)}, f32[32,32,128]{2,1,0:T(8,128)}, u32[]{:S(2)}) copy-start(f32[32,32,128]{2,1,0:T(8,128)} %get-tuple-element.7) | copy-start | bytes 1572868
  48.3 1.2 %copy-start = (f32[8,64,256]{2,1,0:T(8,128)S(1)}, f32[8,64,256]{2,1,0:T(8,128)}, u32[]{:S(2)}) copy-start(f32[8,64,256]{2,1,0:T(8,128)} %get-tuple-element.8) | copy-start | bytes 1572868

commit v4 on v3

--- a/solution.py
+++ b/solution.py
@@ -17,7 +17,8 @@
 STEP_RATIO = 0.088
 EPSILON = 1e-06
 REACH = K - 1
-HALF = SLAB // 2
+PARTS = 4
+HALF = SLAB // PARTS
 SLOTS = 2 * REACH + 1
 OFFSETS = (3, -3, 2, -2, 1, -1)
 MESH = pl.DeviceIdType.MESH
@@ -278,9 +279,9 @@
         index = jnp.clip(d + lag, 0, K - 1)
         return doubled[pl.ds(index * SLAB + half * HALF, HALF), pl.ds(AX - my_cross, AX), :]
 
-    for half in range(2):
+    for half in range(PARTS):
         planes = slice(half * HALF, (half + 1) * HALF)
-        lax.fori_loop(0, AZ // 2, fourth, half, unroll=4)
+        lax.fori_loop(0, AZ // PARTS, fourth, half, unroll=4)
         for d in OFFSETS:
             gsend[d + REACH, planes] = rolled(d, half)
 
@@ -311,8 +312,8 @@
 
         @pl.when(there(d))
         def _(d=d):
-            g_copy(-d, 0).wait_recv()
-            g_copy(-d, 1).wait_recv()
+            for half in range(PARTS):
+                g_copy(-d, half).wait_recv()
             add_piece(d)
 
     largest = jnp.zeros((8, AY), jnp.float32)
@@ -357,8 +358,8 @@
         @pl.when(there(d))
         def _(d=d):
             v_copy(d).wait_send()
-            g_copy(d, 0).wait_send()
-            g_copy(d, 1).wait_send()
+            for half in range(PARTS):
+                g_copy(d, half).wait_send()
 
     wave_store.wait()
     adj_store.wait()
@@ -399,8 +400,8 @@
             dma((2,)),
             dma((SLOTS,)),
             dma((SLOTS,)),
-            dma((2, SLOTS)),
-            dma((2, SLOTS)),
+            dma((PARTS, SLOTS)),
+            dma((PARTS, SLOTS)),
             dma((partners,)),
             dma((partners,)),
         ],

time: 50.5 us -> 49.7 us (0.984)
  Pallas kernels: 45.7 us -> 44.9 us
    pallas_call x1, Pallas kernels: 45.7 us -> 44.9 us  [shards(): pl.pallas_call(functools.partial(kernel, n, stages), out_shape=(jax.Shape...]
where the time goes in v4:
time: 49.7 us; the launch traced here: 49.5 us
  Pallas kernels  44.9 us (90%)
  local copies, waits for them, and re-layouts  3.95 us (8%)
  between operations  0.65 us (1%)
    pallas_call x1, Pallas kernels, shards(): pl.pallas_call(functools.partial(kernel, n, stages), out_shape=(jax.Shape...  44.9 us
    unnamed x7, local copies, waits for them, and re-layouts  3.95 us

profile of v4, /device:TPU:0, one launch (start us, length us, event | category | flops | bytes accessed | tf_op | source)
XLA Modules:
  0.0 49.5 jit_solution(2096516508375934404)
XLA Ops:
  0.6 44.9 %shard_map.112 = (f32[32,32,128]{2,1,0:T(8,128)}, f32[32,32,128]{2,1,0:T(8,128)}, f32[8,64,256]{2,1,0:T(8,128)}) custom-call(f32[8,64,256]{2,1,0:T(8,128)} %vel_in.1, f32[32,32,128]{2,1,0:T(8,128)} %prev_in.1, f32[32,32,128]{2,1,0:T(8,128)} %now_in.1, f32[32,32,128]{2,1,0:T(8,128)} %adj4_in.1, f32[32,32,128]{2,1,0:T(8,128)} %adj3_in.1, f32[1,2]{1,0:T(1,128)} %wavelet.1, ...), custom_call_target="tpu_custom_call" | custom-call | tf_op jit(solution)/shard_map/pallas_call | solution.py:381
  45.5 0.0 copy-start.1
  45.6 1.9 %copy.15 = f32[32,32,128]{2,1,0:T(8,128)} copy(f32[32,32,128]{2,1,0:T(8,128)} %get-tuple-element.6) | data formatting | bytes 1048576
  47.5 0.0 copy-done.1
  47.5 0.0 copy-start
  47.5 0.8 %copy.16 = f32[32,32,128]{2,1,0:T(8,128)} copy(f32[32,32,128]{2,1,0:T(8,128)S(1)} %copy-done.1) | data formatting | bytes 1048576
  48.3 0.4 copy-done
  48.7 0.8 %copy.17 = f32[8,64,256]{2,1,0:T(8,128)} copy(f32[8,64,256]{2,1,0:T(8,128)S(1)} %copy-done) | data formatting | bytes 1048576
Async XLA Ops:
  45.5 1.9 %copy-start.1 = (f32[32,32,128]{2,1,0:T(8,128)S(1)}, f32[32,32,128]{2,1,0:T(8,128)}, u32[]{:S(2)}) copy-start(f32[32,32,128]{2,1,0:T(8,128)} %get-tuple-element.7) | copy-start | bytes 1572868
  47.5 1.2 %copy-start = (f32[8,64,256]{2,1,0:T(8,128)S(1)}, f32[8,64,256]{2,1,0:T(8,128)}, u32[]{:S(2)}) copy-start(f32[8,64,256]{2,1,0:T(8,128)} %get-tuple-element.8) | copy-start | bytes 1572868
